TPU v7x, 32 devices: a whole 2x2x4 slice. The times are simulated.
32 devices in a mesh: gx: 8 (over z, core), gy: 4 (over y, x).
Axes of the slice: x: 2, y: 2, z: 4, core: 2. Of those that a mesh axis runs over, the one named last changes fastest.
Arguments:
- member_flows: float32 [24, 4, 64, 32, 128], P(None, None, 'gx', 'gy'), may hold values from -6 to 6
- wall_texture: float32 [24, 64, 32], P(None, 'gx', 'gy'), may hold values from 0.2 to 2
- cross_link_matrix: float32 [4, 4], replicated, may hold values from -3 to 3
- obs_owner: int32 [4, 4096], replicated, may hold values from 0 to 31
- obs_cell: int32 [4, 4096], replicated, may hold values from 0 to 8191
- obs_value: float32 [4, 4096], replicated, may hold values from -8 to 8
- obs_var: float32 [4, 4096], replicated, may hold values from 0.1 to 1
- local_mask: int32 [4, 8, 4, 64], P(None, 'gx', 'gy'), may hold values 0 or 1
Outputs:
- analysis: float32 [24, 4, 64, 32, 128], P(None, None, 'gx', 'gy')
- rough_post: float32 [24, 64, 32], P(None, 'gx', 'gy')
Inputs may be any that keep to these rules, and one draw needn't show every extreme that they name: `obs_owner`: observations are skewed towards a few tiles.
All inputs are finite; a program needn't handle non-finite values. No bound on the sum of `local_mask` on one device may be relied on, other than what follows from the above.
Results may differ from a plain program's by a relative error of at most 0.0003.
Values sent between devices are 32-bit elements; how exact they have to be, the bound alone decides.
A program may use at most 64 MiB of HBM per device.

v0:
```python
import jax
import jax.numpy as jnp
from jax import lax
from jax.sharding import PartitionSpec as P

BATCHES = 4
OBS_BLOCK = 64


def padded_2(block, sides, width):
    for axis, dim in sides:
        count = lax.axis_size(axis)
        forward = [(i, i + 1) for i in range(count - 1)]
        backward = [(target, source) for source, target in forward]
        low = lax.ppermute(
            lax.slice_in_dim(block, block.shape[dim] - width, None, axis=dim), axis, forward
        )
        high = lax.ppermute(lax.slice_in_dim(block, 0, width, axis=dim), axis, backward)
        block = jnp.concatenate([low, block, high], axis=dim)
    return block


def prior_flow_vector(member_flow_vector, wall_texture_entries, cross_link_matrix):
    padded = padded_2(member_flow_vector, (("gx", 2), ("gy", 3)), 1)
    padded = jnp.pad(padded, ((0, 0), (0, 0), (0, 0), (0, 0), (1, 1)))
    center = padded[:, :, 1:-1, 1:-1, 1:-1]
    lap = padded[:, :, 2:, 1:-1, 1:-1] + padded[:, :, :-2, 1:-1, 1:-1]
    lap = lap + padded[:, :, 1:-1, 2:, 1:-1] + padded[:, :, 1:-1, :-2, 1:-1]
    lap = lap + padded[:, :, 1:-1, 1:-1, 2:] + padded[:, :, 1:-1, 1:-1, :-2] - 6.0 * center
    slope = 0.5 * (padded[:, :, 2:, 1:-1, 1:-1] - padded[:, :, :-2, 1:-1, 1:-1])
    mixed = jnp.einsum(
        "fg,mgxyz->mfxyz", cross_link_matrix, center, precision=lax.Precision.HIGHEST
    )
    level = (lax.broadcasted_iota(jnp.int32, (center.shape[-1],), 0) == 0).astype(jnp.float32)
    drag = wall_texture_entries[:, None, :, :, None] * center * level
    return center + 0.5 * (0.15 * lap - 0.6 * slope + mixed - drag)


def observation_terms(values, value_b, var_b):
    members = values.shape[0]
    ybar = jnp.mean(values, axis=0)
    dev = values - ybar[None, :]
    spread = jnp.sum(dev * dev, axis=0) / (members - 1.0)
    root = jnp.sqrt(spread + var_b)
    gterm = ((value_b - ybar) / (spread + var_b))[None, :] - dev / (
        root * (jnp.sqrt(var_b) + root)
    )[None, :]
    return (dev, gterm)


def apply_mixing(member_flow_vector, wall_texture_entries, mixing):
    flat_state = member_flow_vector.reshape(member_flow_vector.shape[0], -1)
    prime = flat_state - jnp.mean(flat_state, axis=0, keepdims=True)
    member_flow_vector = (
        flat_state + jnp.dot(mixing.T, prime, precision=lax.Precision.HIGHEST)
    ).reshape(member_flow_vector.shape)
    flat_rough = wall_texture_entries.reshape(wall_texture_entries.shape[0], -1)
    rprime = flat_rough - jnp.mean(flat_rough, axis=0, keepdims=True)
    wall_texture_entries = (
        flat_rough + jnp.dot(mixing.T, rprime, precision=lax.Precision.HIGHEST)
    ).reshape(wall_texture_entries.shape)
    return (member_flow_vector, wall_texture_entries)


def on_device(
    member_flows,
    wall_texture,
    cross_link_matrix,
    obs_owner,
    obs_cell,
    obs_value,
    obs_var,
    local_mask,
):
    members = member_flows.shape[0]
    cells = member_flows.shape[2] * member_flows.shape[3] * member_flows.shape[4]
    member_flow_vector = prior_flow_vector(member_flows, wall_texture, cross_link_matrix)
    wall_texture_entries = wall_texture
    mytile = lax.axis_index("gx") * lax.axis_size("gy") + lax.axis_index("gy")
    for batch in range(BATCHES):
        flat_first = member_flow_vector[:, 0].reshape(members, cells)
        picked = jnp.take(flat_first, obs_cell[batch], axis=1)
        owned = (obs_owner[batch] == mytile)[None, :]
        local_vals = jnp.where(owned, picked, 0.0)
        block_weight = local_mask[batch, 0, 0].astype(jnp.float32)
        values = lax.psum(local_vals, ("gx", "gy"))
        dev, gterm = observation_terms(values, obs_value[batch], obs_var[batch])
        weighted = dev * jnp.repeat(block_weight, OBS_BLOCK)[None, :]
        mixing = jnp.dot(weighted, gterm.T, precision=lax.Precision.HIGHEST) / (members - 1.0)
        member_flow_vector, wall_texture_entries = apply_mixing(
            member_flow_vector, wall_texture_entries, mixing
        )
    return (member_flow_vector, wall_texture_entries)


def solution(mesh):
    return jax.shard_map(
        on_device,
        mesh=mesh,
        in_specs=(
            P(None, None, "gx", "gy", None),
            P(None, "gx", "gy"),
            P(),
            P(),
            P(),
            P(),
            P(),
            P(None, "gx", "gy", None),
        ),
        out_specs=(P(None, None, "gx", "gy", None), P(None, "gx", "gy")),
        check_vma=False,
    )
```

profile of v0, /device:TPU:0, one launch (start us, length us, event | category | flops | bytes accessed | tf_op | source)
XLA Modules:
  0.0 787.6 jit_solution(4160225619469467906)
XLA Ops:
  7.3 4.5 copy.87
  29.2 4.9 collective-permute-start.3
  37.4 4.0 collective-permute-done.2
  43.1 9.1 %select_maximum_fusion = f32[24,4,10,10,130]{4,1,3,2,0:T(4,128)S(1)} fusion(f32[24,4,10,1,128]{4,1,3,2,0:T(4,128)S(1)} %collective-permute-done.2, f32[24,4,10,8,128]{4,1,3,2,0:T(4,128)} %copy-done.9, f32[24,4,10,1,128]{4,1,3,2,0:T(4,128)S(1)} %collective-permute-done.3), kind=kLoop, calls=%fused_computation.10 | loop fusion | flops 9984000 | bytes 9907200 | tf_op jit(solution)/shard_map/concatenate | solution.py:19
  52.3 13.3 %fusion.94 = (f32[4,8,8,128]{3,0,2,1:T(4,128)S(1)}, f32[24,4,8,8,128]{4,1,3,2,0:T(4,128)S(1)}) fusion(f32[24,4,8,8,128]{4,1,3,2,0:T(4,128)S(1)} %copy-done.12, f32[128]{0:T(128)S(1)} %compare_convert_fusion, f32[24,8,8]{2,1,0:T(8,128)S(1)} %copy.85, f32[4,4]{1,0:T(4,128)S(1)} %copy-done, f32[24,4,10,10,130]{4,1,3,2,0:T(4,128)S(1)} %select_maximum_fusion, ...), kind=kOutput, calls=%fused_computation.155 | convolution fusion | flops 55017472 | bytes 21662208 | tf_op jit(solution)/shard_map/fg,mgxyz->mfxyz/dot_general | solution.py:31
  67.7 4.6 copy.97
  72.3 16.4 %gather_fusion = f32[4096,24]{1,0:T(8,128)} fusion(f32[24,8192]{0,1:T(8,128)} %bitcast.91, s32[4096]{0:T(1024)S(1)} %fusion.79), kind=kCustom, calls=%fused_computation.clone | custom fusion | bytes 802816 | tf_op jit(solution)/shard_map/jit(_take)/gather | solution.py:82
  88.7 6.0 bitcast_select_fusion.3
  94.9 148.3 %all-reduce.6.cloned.1.call-done = f32[24,4096]{0,1:T(8,128)} async-done(((f32[24,4096]{0,1:T(8,128)}), f32[24,4096]{0,1:T(8,128)}) %all-reduce.6.cloned.1.call-update) | async-done | bytes 393232 | tf_op jit(solution)/shard_map/psum | solution.py:86
  248.9 8.3 %fusion.41 = f32[24,24]{1,0:T(8,128)S(1)} fusion(f32[24,4096]{0,1:T(8,128)} %all-reduce.6.cloned.1.call-done, f32[4096]{0:T(1024)S(1)} %bitcast.120, f32[4096]{0:T(1024)S(1)} %bitcast.119, f32[4096]{0:T(1024)S(1)} %mul.121, f32[4096]{0:T(1024)S(1)} %broadcast_multiply_fusion.10), kind=kOutput, calls=%fused_computation.70 | convolution fusion | flops 28803648 | bytes 461056 | tf_op jit(solution)/shard_map/dot_general | solution.py:89
  257.2 6.3 fusion.95
  267.9 13.0 %gather_fusion.1 = f32[4096,24]{1,0:T(8,128)S(1)} fusion(f32[24,8192]{0,1:T(8,128)} %bitcast.92, s32[4096]{0:T(1024)S(1)} %fusion.80), kind=kCustom, calls=%fused_computation.1.clone | custom fusion | bytes 802816 | tf_op jit(solution)/shard_map/jit(_take)/gather | solution.py:82
  284.7 131.7 %all-reduce.8.cloned.1.call-done = f32[24,4096]{0,1:T(8,128)} async-done(((f32[24,4096]{0,1:T(8,128)}), f32[24,4096]{0,1:T(8,128)}) %all-reduce.8.cloned.1.call-update) | async-done | bytes 393232 | tf_op jit(solution)/shard_map/psum | solution.py:86
  421.1 6.2 fusion.46
  427.4 3.4 fusion.96
  432.3 3.6 copy.92
  435.9 16.4 %gather_fusion.2 = f32[4096,24]{1,0:T(8,128)} fusion(f32[24,8192]{0,1:T(8,128)} %bitcast.93, s32[4096]{0:T(1024)S(1)} %fusion.81), kind=kCustom, calls=%fused_computation.2.clone | custom fusion | bytes 802816 | tf_op jit(solution)/shard_map/jit(_take)/gather | solution.py:82
  452.2 6.0 bitcast_select_fusion.1
  458.8 132.2 %all-reduce.10.cloned.1.call-done = f32[24,4096]{0,1:T(8,128)} async-done(((f32[24,4096]{0,1:T(8,128)}), f32[24,4096]{0,1:T(8,128)}) %all-reduce.10.cloned.1.call-update) | async-done | bytes 393232 | tf_op jit(solution)/shard_map/psum | solution.py:86
  596.7 8.3 %fusion.51 = f32[24,24]{1,0:T(8,128)S(1)} fusion(f32[24,4096]{0,1:T(8,128)} %all-reduce.10.cloned.1.call-done, f32[4096]{0:T(1024)S(1)} %bitcast.124, f32[4096]{0:T(1024)S(1)} %bitcast.123, f32[4096]{0:T(1024)} %mul.131, f32[4096]{0:T(1024)S(1)} %broadcast_multiply_fusion.8), kind=kOutput, calls=%fused_computation.72 | convolution fusion | flops 28803648 | bytes 461056 | tf_op jit(solution)/shard_map/dot_general | solution.py:89
  605.1 3.4 fusion.97
  612.8 13.0 %gather_fusion.3 = f32[4096,24]{1,0:T(8,128)S(1)} fusion(f32[24,8192]{0,1:T(8,128)} %bitcast.94, s32[4096]{0:T(1024)S(1)} %fusion.82), kind=kCustom, calls=%fused_computation.3.clone | custom fusion | bytes 802816 | tf_op jit(solution)/shard_map/jit(_take)/gather | solution.py:82
  628.7 132.5 %all-reduce.12.cloned.1.call-done = f32[24,4096]{0,1:T(8,128)} async-done(((f32[24,4096]{0,1:T(8,128)}), f32[24,4096]{0,1:T(8,128)}) %all-reduce.12.cloned.1.call-update) | async-done | bytes 393232 | tf_op jit(solution)/shard_map/psum | solution.py:86
  766.0 8.8 %fusion.56 = f32[24,24]{1,0:T(8,128)S(1)} fusion(f32[24,4096]{0,1:T(8,128)} %all-reduce.12.cloned.1.call-done, f32[4096]{0:T(1024)S(1)} %bitcast.126, f32[4096]{0:T(1024)S(1)} %bitcast.125, f32[4096]{0:T(1024)S(1)} %copy-done.20, f32[4096]{0:T(1024)S(1)} %broadcast_multiply_fusion.7), kind=kOutput, calls=%fused_computation.73 | convolution fusion | flops 28803648 | bytes 461056 | tf_op jit(solution)/shard_map/dot_general | solution.py:89
  (148 shorter events, 68.9 us)
Async XLA Ops:
  7.2 45.1 %copy-start = (f32[4,4]{1,0:T(4,128)S(1)}, f32[4,4]{1,0:T(4,128)}, u32[]{:S(2)}) copy-start(f32[4,4]{1,0:T(4,128)} %param.12) | copy-start | bytes 196
  7.2 14.9 %copy-start.6 = (f32[24,4,8,8,128]{4,3,2,1,0:T(8,128)S(1)}, f32[24,4,8,8,128]{4,3,2,1,0:T(8,128)}, u32[]{:S(2)}) copy-start(f32[24,4,8,8,128]{4,3,2,1,0:T(8,128)} %param.10) | copy-start | bytes 9437188
  7.2 11.6 %copy-start.15 = (s32[4,4096]{1,0:T(4,128)S(1)}, s32[4,4096]{1,0:T(4,128)}, u32[]{:S(2)}) copy-start(s32[4,4096]{1,0:T(4,128)} %param.14) | copy-start | bytes 196612
  7.2 11.7 %copy-start.13 = (f32[24,8,8]{0,2,1:T(8,128)S(1)}, f32[24,8,8]{0,2,1:T(8,128)}, u32[]{:S(2)}) copy-start(f32[24,8,8]{0,2,1:T(8,128)} %param.11) | copy-start | bytes 18436
  7.2 13.0 %copy-start.28 = (s32[4,1,1,64]{3,2,1,0:T(1,128)S(1)}, s32[4,1,1,64]{3,2,1,0:T(1,128)}, u32[]{:S(2)}) copy-start(s32[4,1,1,64]{3,2,1,0:T(1,128)} %param.17) | copy-start | bytes 3076
  7.2 13.0 %copy-start.14 = (s32[4,4096]{1,0:T(4,128)S(1)}, s32[4,4096]{1,0:T(4,128)}, u32[]{:S(2)}) copy-start(s32[4,4096]{1,0:T(4,128)} %param.13) | copy-start | bytes 196612
  7.2 236.0 %all-reduce.6.cloned.1.call-start = ((), (), s32[]{:S(2)}) async-start(), calls=%async_computation | async-start | bytes 4194304 | tf_op jit(solution)/shard_map/psum | solution.py:86
  14.4 6.6 collective-permute-start.1
  17.5 7.3 collective-permute-start
  27.9 13.4 %collective-permute-start.2 = (f32[24,4,10,1,128]{4,1,3,2,0:T(4,128)S(1)}, f32[24,4,10,1,128]{4,1,3,2,0:T(4,128)S(1)}, u32[]{:S(2)}, u32[]{:S(2)}) collective-permute-start(f32[24,4,10,1,128]{4,1,3,2,0:T(4,128)S(1)} %get-tuple-element.10), channel_id=1, source_target_pairs={{1,0},{2,1},{3,2},{5,4},{6,5},{7,6},{9,8},{10,9},{11,10},{13,12},{... | collective-permute-start | bytes 1474568 | tf_op jit(solution)/shard_map/ppermute | solution.py:18
  29.2 13.9 %collective-permute-start.3 = (f32[24,4,10,1,128]{4,1,3,2,0:T(4,128)S(1)}, f32[24,4,10,1,128]{4,1,3,2,0:T(4,128)S(1)}, u32[]{:S(2)}, u32[]{:S(2)}) collective-permute-start(f32[24,4,10,1,128]{4,1,3,2,0:T(4,128)S(1)} %get-tuple-element.9), channel_id=1, source_target_pairs={{0,1},{1,2},{2,3},{4,5},{5,6},{6,7},{8,9},{9,10},{10,11},{12,13},{... | collective-permute-start | bytes 1474568 | tf_op jit(solution)/shard_map/ppermute | solution.py:15
  37.4 14.9 %copy-start.10 = (f32[24,4,10,8,128]{4,1,3,2,0:T(4,128)S(1)}, f32[24,4,10,8,128]{4,1,3,2,0:T(4,128)}, u32[]{:S(2)}) copy-start(f32[24,4,10,8,128]{4,1,3,2,0:T(4,128)} %copy-done.9) | copy-start | bytes 11796484
  37.4 14.9 %copy-start.12 = (f32[24,4,8,8,128]{4,1,3,2,0:T(4,128)S(1)}, f32[24,4,8,8,128]{4,1,3,2,0:T(4,128)}, u32[]{:S(2)}) copy-start(f32[24,4,8,8,128]{4,1,3,2,0:T(4,128)} %copy-done.11) | copy-start | bytes 9437188
  94.6 321.8 %all-reduce.8.cloned.1.call-start = ((), (), s32[]{:S(2)}) async-start(), calls=%async_computation.1 | async-start | bytes 4194304 | tf_op jit(solution)/shard_map/psum | solution.py:86
  265.3 15.6 %copy-start.26 = (pred[4096]{0:T(1024)(128)(4,1)S(1)}, pred[4096]{0:T(1024)(128)(4,1)}, u32[]{:S(2)}) copy-start(pred[4096]{0:T(1024)(128)(4,1)} %get-tuple-element.6) | copy-start | bytes 12292
  283.5 136.6 %copy-start.16 = (f32[4,4096]{1,0:T(4,128)S(1)}, f32[4,4096]{1,0:T(4,128)}, u32[]{:S(2)}) copy-start(f32[4,4096]{1,0:T(4,128)} %param.15) | copy-start | bytes 196612
  283.6 137.5 %copy-start.21 = (f32[4096]{0:T(1024)S(1)}, f32[4096]{0:T(1024)}, u32[]{:S(2)}) copy-start(f32[4096]{0:T(1024)} %mul.126) | copy-start | bytes 49156
  283.6 307.5 %all-reduce.10.cloned.1.call-start = ((), (), s32[]{:S(2)}) async-start(), calls=%async_computation.2 | async-start | bytes 4194304 | tf_op jit(solution)/shard_map/psum | solution.py:86
  432.3 19.9 %copy-start.24 = (pred[4096]{0:T(1024)(128)(4,1)S(1)}, pred[4096]{0:T(1024)(128)(4,1)}, u32[]{:S(2)}) copy-start(pred[4096]{0:T(1024)(128)(4,1)} %compare_and_fusion.1) | copy-start | bytes 12292
  432.3 19.9 %copy-start.25 = (pred[4096]{0:T(1024)(128)(4,1)S(1)}, pred[4096]{0:T(1024)(128)(4,1)}, u32[]{:S(2)}) copy-start(pred[4096]{0:T(1024)(128)(4,1)} %get-tuple-element.8) | copy-start | bytes 12292
  458.2 303.0 %all-reduce.12.cloned.1.call-start = ((), (), s32[]{:S(2)}) async-start(), calls=%async_computation.3 | async-start | bytes 4194304 | tf_op jit(solution)/shard_map/psum | solution.py:86
  610.2 15.6 %copy-start.22 = (pred[4096]{0:T(1024)(128)(4,1)S(1)}, pred[4096]{0:T(1024)(128)(4,1)}, u32[]{:S(2)}) copy-start(pred[4096]{0:T(1024)(128)(4,1)} %compare_and_fusion) | copy-start | bytes 12292
  610.2 15.6 %copy-start.23 = (pred[4096]{0:T(1024)(128)(4,1)S(1)}, pred[4096]{0:T(1024)(128)(4,1)}, u32[]{:S(2)}) copy-start(pred[4096]{0:T(1024)(128)(4,1)} %get-tuple-element.5) | copy-start | bytes 12292
  628.5 137.5 %copy-start.20 = (f32[4096]{0:T(1024)S(1)}, f32[4096]{0:T(1024)}, u32[]{:S(2)}) copy-start(f32[4096]{0:T(1024)} %mul.136) | copy-start | bytes 49156
  (13 other events, 51.5 us)
Sparse Core Ops, SparseCore 0:
  94.8 148.4 all-reduce.5
  283.7 132.6 all-reduce.7
  458.4 132.6 all-reduce.9
  628.6 132.6 all-reduce.11
where the time goes:
time: 797 us; the launch traced here: 788 us
  waiting for transfers between devices  551 us (69%)
  local copies, waits for them, and re-layouts  99.2 us (12%)
  matrix products  62.7 us (8%)
  other arithmetic  49.2 us (6%)
  between operations  14.7 us (2%)
  starting transfers between devices  11.4 us (1%)
    psum x4, waiting for transfers between devices, on_device(): values = lax.psum(local_vals, ('gx', 'gy'))  545 us
    gather x4, local copies, waits for them, and re-layouts, on_device(): picked = jnp.take(flat_first, obs_cell[batch], axis=1)  58.7 us
    dot_general x4, matrix products, on_device(): jnp.dot(weighted, gterm.T, precision=lax.Precision.HIGHEST)  31.6 us
    unnamed x66, local copies, waits for them, and re-layouts  18.1 us
    select_n x4, other arithmetic, on_device(): local_vals = jnp.where(owned, picked, 0.0)  17.3 us
    dot_general x4, matrix products, apply_mixing(): jnp.dot(mixing.T, prime, precision=lax.Precision.HIGHEST)  16.2 us
  transfers between devices with their start and end apart: 8, of which 6 were waited for; matrix products, arithmetic and copies ran while one was open for 1% of the time, Pallas kernels for 0%

commit v1 on v0

--- a/solution.py
+++ b/solution.py
@@ -83,7 +83,7 @@
         owned = (obs_owner[batch] == mytile)[None, :]
         local_vals = jnp.where(owned, picked, 0.0)
         block_weight = local_mask[batch, 0, 0].astype(jnp.float32)
-        values = lax.psum(local_vals, ("gx", "gy"))
+        values = jnp.sum(lax.all_gather(local_vals, ("gx", "gy")), axis=0)
         dev, gterm = observation_terms(values, obs_value[batch], obs_var[batch])
         weighted = dev * jnp.repeat(block_weight, OBS_BLOCK)[None, :]
         mixing = jnp.dot(weighted, gterm.T, precision=lax.Precision.HIGHEST) / (members - 1.0)

time: 797 us -> 663 us (0.83)
  waiting for transfers between devices: 551 us -> 392 us
  other arithmetic: 49.2 us -> 81 us
  matrix products: 62.7 us -> 40.3 us
  local copies, waits for them, and re-layouts: 99.2 us -> 115 us
    psum x4 -> x0, waiting for transfers between devices: 545 us -> none  [on_device(): values = lax.psum(local_vals, ('gx', 'gy'))]
    all_gather x0 -> x4, waiting for transfers between devices: none -> 384 us  [on_device(): values = jnp.sum(lax.all_gather(local_vals, ('gx', 'gy')), axis=0)]
    dot_general x4, matrix products: 31.6 us -> 4.51 us  [on_device(): jnp.dot(weighted, gterm.T, precision=lax.Precision.HIGHEST)]
    reduce_sum x0 -> x4, other arithmetic: none -> 20.8 us  [on_device(): values = jnp.sum(lax.all_gather(local_vals, ('gx', 'gy')), axis=0)]
    reduce_sum x4, other arithmetic: 9.09 us -> 22.1 us  [observation_terms(): ybar = jnp.mean(values, axis=0)]
    unnamed x66 -> x74, local copies, waits for them, and re-layouts: 18.1 us -> 20.1 us
  transfers between devices with their start and end apart: 8 -> 8, of which waited for: 6 -> 6; matrix products, arithmetic and copies ran while one was open for 1% -> 2% of each run, Pallas kernels for 0% -> 0%
where the time goes in v1:
time: 663 us; the launch traced here: 653 us
  waiting for transfers between devices  392 us (59%)
  local copies, waits for them, and re-layouts  115 us (17%)
  other arithmetic  81 us (12%)
  matrix products  40.3 us (6%)
  between operations  14.7 us (2%)
  starting transfers between devices  10.6 us (2%)
    all_gather x4, waiting for transfers between devices, on_device(): values = jnp.sum(lax.all_gather(local_vals, ('gx', 'gy')), axis=0)  384 us
    gather x4, local copies, waits for them, and re-layouts, on_device(): picked = jnp.take(flat_first, obs_cell[batch], axis=1)  65.2 us
    reduce_sum x4, other arithmetic, observation_terms(): ybar = jnp.mean(values, axis=0)  22.1 us
    dot_general x4, matrix products, apply_mixing(): jnp.dot(mixing.T, prime, precision=lax.Precision.HIGHEST)  21.6 us
    reduce_sum x4, other arithmetic, on_device(): values = jnp.sum(lax.all_gather(local_vals, ('gx', 'gy')), axis=0)  20.8 us
    unnamed x74, local copies, waits for them, and re-layouts  20.1 us
    select_n x4, other arithmetic, on_device(): local_vals = jnp.where(owned, picked, 0.0)  15.5 us
  transfers between devices with their start and end apart: 8, of which 6 were waited for; matrix products, arithmetic and copies ran while one was open for 2% of the time, Pallas kernels for 0%

profile of v1, /device:TPU:0, one launch (start us, length us, event | category | flops | bytes accessed | tf_op | source)
XLA Modules:
  0.0 653.5 jit_solution(10514645233891234021)
XLA Ops:
  7.2 4.6 copy.121
  28.5 4.9 collective-permute-start.3
  33.6 6.3 collective-permute-done.2
  41.7 9.1 %select_maximum_fusion = f32[24,4,10,10,130]{4,1,3,2,0:T(4,128)S(1)} fusion(f32[24,4,10,1,128]{4,1,3,2,0:T(4,128)S(1)} %collective-permute-done.2, f32[24,4,10,8,128]{4,1,3,2,0:T(4,128)} %copy-done.6, f32[24,4,10,1,128]{4,1,3,2,0:T(4,128)S(1)} %collective-permute-done.3), kind=kLoop, calls=%fused_computation.10 | loop fusion | flops 9984000 | bytes 9907200 | tf_op jit(solution)/shard_map/concatenate | solution.py:19
  50.9 13.2 %fusion.70 = (f32[4,8,8,128]{3,0,2,1:T(4,128)S(1)}, f32[24,4,8,8,128]{4,1,3,2,0:T(4,128)S(1)}) fusion(f32[24,4,8,8,128]{4,1,3,2,0:T(4,128)S(1)} %copy-done.9, f32[128]{0:T(128)S(1)} %compare_convert_fusion, f32[24,8,8]{2,1,0:T(8,128)S(1)} %copy.119, f32[4,4]{1,0:T(4,128)S(1)} %copy-done, f32[24,4,10,10,130]{4,1,3,2,0:T(4,128)S(1)} %select_maximum_fusion, ...), kind=kOutput, calls=%fused_computation.151 | convolution fusion | flops 55017472 | bytes 21662208 | tf_op jit(solution)/shard_map/fg,mgxyz->mfxyz/dot_general | solution.py:31
  69.6 16.3 %gather_fusion = f32[4096,24]{1,0:T(8,128)} fusion(f32[24,8192]{0,1:T(8,128)} %bitcast.99, s32[4096]{0:T(1024)S(1)} %fusion.55), kind=kCustom, calls=%fused_computation.clone | custom fusion | bytes 802816 | tf_op jit(solution)/shard_map/jit(_take)/gather | solution.py:82
  96.0 106.6 %all-gather.9.cloned.1.call-done = f32[768,4096]{1,0:T(8,128)} async-done(((f32[24,4096]{1,0:T(8,128)}), f32[768,4096]{1,0:T(8,128)}) %all-gather.9.cloned.1.call-update) | async-done | bytes 12582928 | tf_op jit(solution)/shard_map/all_gather | solution.py:86
  202.6 5.2 reduce_sum.181
  208.4 5.2 reduce_sum.180
  216.8 7.3 %fusion.71 = (f32[32768]{0:T(1024)S(1)}, f32[24,32768]{1,0:T(8,128)S(1)}) fusion(f32[24,24]{1,0:T(8,128)S(1)} %convolution_multiply_fusion.3, f32[3,8,256,128]{3,2,1,0:T(8,128)S(1)} %bitcast.103, f32[32768]{0:T(1024)} %bitcast.108), kind=kOutput, calls=%fused_computation.152 | convolution fusion | flops 228818944 | bytes 6555904 | tf_op jit(solution)/shard_map/dot_general | solution.py:55
  228.5 16.3 %gather_fusion.1 = f32[4096,24]{1,0:T(8,128)} fusion(f32[24,8192]{0,1:T(8,128)} %bitcast.100, s32[4096]{0:T(1024)S(1)} %copy-done.19), kind=kCustom, calls=%fused_computation.1.clone | custom fusion | bytes 802816 | tf_op jit(solution)/shard_map/jit(_take)/gather | solution.py:82
  249.7 93.9 %all-gather.11.cloned.1.call-done = f32[768,4096]{1,0:T(8,128)} async-done(((f32[24,4096]{1,0:T(8,128)}), f32[768,4096]{1,0:T(8,128)}) %all-gather.11.cloned.1.call-update) | async-done | bytes 12582928 | tf_op jit(solution)/shard_map/all_gather | solution.py:86
  343.7 5.2 reduce_sum.184
  348.9 5.2 reduce_sum.185
  355.7 6.0 fusion.72
  366.7 16.4 %gather_fusion.2 = f32[4096,24]{1,0:T(8,128)} fusion(f32[24,8192]{0,1:T(8,128)} %bitcast.101, s32[4096]{0:T(1024)S(1)} %fusion.57), kind=kCustom, calls=%fused_computation.2.clone | custom fusion | bytes 802816 | tf_op jit(solution)/shard_map/jit(_take)/gather | solution.py:82
  383.1 6.0 bitcast_select_fusion.1
  394.7 91.7 %all-gather.13.cloned.1.call-done = f32[768,4096]{1,0:T(8,128)} async-done(((f32[24,4096]{1,0:T(8,128)}), f32[768,4096]{1,0:T(8,128)}) %all-gather.13.cloned.1.call-update) | async-done | bytes 12582928 | tf_op jit(solution)/shard_map/all_gather | solution.py:86
  486.5 5.2 reduce_sum.188
  491.7 5.8 reduce_sum.189
  509.4 16.3 %gather_fusion.3 = f32[4096,24]{1,0:T(8,128)} fusion(f32[24,8192]{0,1:T(8,128)} %bitcast.102, s32[4096]{0:T(1024)S(1)} %copy-done.20), kind=kCustom, calls=%fused_computation.3.clone | custom fusion | bytes 802816 | tf_op jit(solution)/shard_map/jit(_take)/gather | solution.py:82
  532.8 91.9 %all-gather.15.cloned.1.call-done = f32[768,4096]{1,0:T(8,128)} async-done(((f32[24,4096]{1,0:T(8,128)}), f32[768,4096]{1,0:T(8,128)}) %all-gather.15.cloned.1.call-update) | async-done | bytes 12582928 | tf_op jit(solution)/shard_map/all_gather | solution.py:86
  624.7 5.2 reduce_sum.192
  629.9 5.9 reduce_sum.193
  (164 shorter events, 89.1 us)
Async XLA Ops:
  7.2 43.7 %copy-start = (f32[4,4]{1,0:T(4,128)S(1)}, f32[4,4]{1,0:T(4,128)}, u32[]{:S(2)}) copy-start(f32[4,4]{1,0:T(4,128)} %param.12) | copy-start | bytes 196
  7.2 14.2 %copy-start.5 = (f32[24,4,8,8,128]{4,3,2,1,0:T(8,128)S(1)}, f32[24,4,8,8,128]{4,3,2,1,0:T(8,128)}, u32[]{:S(2)}) copy-start(f32[24,4,8,8,128]{4,3,2,1,0:T(8,128)} %param.10) | copy-start | bytes 9437188
  7.2 195.4 %all-gather.9.cloned.1.call-start = ((), (), s32[]{:S(2)}) async-start(), calls=%async_computation | async-start | bytes 12976128 | tf_op jit(solution)/shard_map/all_gather | solution.py:86
  7.2 10.9 %copy-start.21 = (s32[4,4096]{1,0:T(4,128)S(1)}, s32[4,4096]{1,0:T(4,128)}, u32[]{:S(2)}) copy-start(s32[4,4096]{1,0:T(4,128)} %param.14) | copy-start | bytes 196612
  14.4 6.1 collective-permute-start.1
  16.8 7.3 %collective-permute-start = (f32[24,4,1,8,128]{4,1,3,2,0:T(4,128)}, f32[24,4,1,8,128]{4,1,3,2,0:T(4,128)}, u32[]{:S(2)}, u32[]{:S(2)}) collective-permute-start(f32[24,4,1,8,128]{4,1,3,2,0:T(4,128)} %get-tuple-element.11), channel_id=1, source_target_pairs={{4,0},{8,4},{12,8},{16,12},{20,16},{24,20},{28,24},{5,1},{9,5},{13... | collective-permute-start | bytes 1179656 | tf_op jit(solution)/shard_map/ppermute | solution.py:18
  21.3 12.1 %copy-start.11 = (f32[24,8,8]{0,2,1:T(8,128)S(1)}, f32[24,8,8]{0,2,1:T(8,128)}, u32[]{:S(2)}) copy-start(f32[24,8,8]{0,2,1:T(8,128)} %param.11) | copy-start | bytes 18436
  21.4 12.2 %copy-start.18 = (s32[1,4096]{1,0:T(1,128)S(1)}, s32[1,4096]{1,0:T(1,128)}, u32[]{:S(2)}) copy-start(s32[1,4096]{1,0:T(1,128)} %get-tuple-element.23) | copy-start | bytes 49156
  27.2 12.7 %collective-permute-start.2 = (f32[24,4,10,1,128]{4,1,3,2,0:T(4,128)S(1)}, f32[24,4,10,1,128]{4,1,3,2,0:T(4,128)S(1)}, u32[]{:S(2)}, u32[]{:S(2)}) collective-permute-start(f32[24,4,10,1,128]{4,1,3,2,0:T(4,128)S(1)} %get-tuple-element.10), channel_id=1, source_target_pairs={{1,0},{2,1},{3,2},{5,4},{6,5},{7,6},{9,8},{10,9},{11,10},{13,12},{... | collective-permute-start | bytes 1474568 | tf_op jit(solution)/shard_map/ppermute | solution.py:18
  28.5 13.2 %collective-permute-start.3 = (f32[24,4,10,1,128]{4,1,3,2,0:T(4,128)S(1)}, f32[24,4,10,1,128]{4,1,3,2,0:T(4,128)S(1)}, u32[]{:S(2)}, u32[]{:S(2)}) collective-permute-start(f32[24,4,10,1,128]{4,1,3,2,0:T(4,128)S(1)} %get-tuple-element.9), channel_id=1, source_target_pairs={{0,1},{1,2},{2,3},{4,5},{5,6},{6,7},{8,9},{9,10},{10,11},{12,13},{... | collective-permute-start | bytes 1474568 | tf_op jit(solution)/shard_map/ppermute | solution.py:15
  33.6 17.3 %copy-start.7 = (f32[24,4,10,8,128]{4,1,3,2,0:T(4,128)S(1)}, f32[24,4,10,8,128]{4,1,3,2,0:T(4,128)}, u32[]{:S(2)}) copy-start(f32[24,4,10,8,128]{4,1,3,2,0:T(4,128)} %copy-done.6) | copy-start | bytes 11796484
  33.6 17.3 %copy-start.9 = (f32[24,4,8,8,128]{4,1,3,2,0:T(4,128)S(1)}, f32[24,4,8,8,128]{4,1,3,2,0:T(4,128)}, u32[]{:S(2)}) copy-start(f32[24,4,8,8,128]{4,1,3,2,0:T(4,128)} %copy-done.8) | copy-start | bytes 9437188
  33.6 17.3 %copy-start.14 = (f32[24,4,1,8,128]{4,1,3,2,0:T(4,128)S(1)}, f32[24,4,1,8,128]{4,1,3,2,0:T(4,128)}, u32[]{:S(2)}) copy-start(f32[24,4,1,8,128]{4,1,3,2,0:T(4,128)} %copy-done.13) | copy-start | bytes 1179652
  85.9 6.4 copy-start.17
  90.5 253.2 %all-gather.11.cloned.1.call-start = ((), (), s32[]{:S(2)}) async-start(), calls=%async_computation.1 | async-start | bytes 12976128 | tf_op jit(solution)/shard_map/all_gather | solution.py:86
  216.8 7.3 %copy-start.25 = (f32[24,24]{1,0:T(8,128)}, f32[24,24]{1,0:T(8,128)S(1)}, u32[]{:S(2)}) copy-start(f32[24,24]{1,0:T(8,128)S(1)} %convolution_multiply_fusion.3) | copy-start | bytes 6916
  249.3 237.1 %all-gather.13.cloned.1.call-start = ((), (), s32[]{:S(2)}) async-start(), calls=%async_computation.2 | async-start | bytes 12976128 | tf_op jit(solution)/shard_map/all_gather | solution.py:86
  363.2 19.9 %copy-start.28 = (pred[4096]{0:T(1024)(128)(4,1)S(1)}, pred[4096]{0:T(1024)(128)(4,1)}, u32[]{:S(2)}) copy-start(pred[4096]{0:T(1024)(128)(4,1)} %get-tuple-element.8) | copy-start | bytes 12292
  383.1 9.0 %copy-start.31 = (f32[64]{0:T(128)S(1)}, f32[64]{0:T(128)}, u32[]{:S(2)}) copy-start(f32[64]{0:T(128)} %get-tuple-element.28) | copy-start | bytes 772
  383.1 9.8 %copy-start.15 = (s32[1,4096]{1,0:T(1,128)S(1)}, s32[1,4096]{1,0:T(1,128)}, u32[]{:S(2)}) copy-start(s32[1,4096]{1,0:T(1,128)} %get-tuple-element.21) | copy-start | bytes 49156
  392.0 232.6 %all-gather.15.cloned.1.call-start = ((), (), s32[]{:S(2)}) async-start(), calls=%async_computation.3 | async-start | bytes 12976128 | tf_op jit(solution)/shard_map/all_gather | solution.py:86
  506.6 19.1 %copy-start.27 = (pred[4096]{0:T(1024)(128)(4,1)S(1)}, pred[4096]{0:T(1024)(128)(4,1)}, u32[]{:S(2)}) copy-start(pred[4096]{0:T(1024)(128)(4,1)} %get-tuple-element.5) | copy-start | bytes 12292
  506.6 19.1 %copy-start.29 = (pred[4096]{0:T(1024)(128)(4,1)S(1)}, pred[4096]{0:T(1024)(128)(4,1)}, u32[]{:S(2)}) copy-start(pred[4096]{0:T(1024)(128)(4,1)} %compare_and_fusion) | copy-start | bytes 12292
  629.9 10.5 %copy-start.4 = (f32[24,32768]{1,0:T(8,128)S(1)}, f32[24,32768]{1,0:T(8,128)}, u32[]{:S(2)}) copy-start(f32[24,32768]{1,0:T(8,128)} %copy-done.3) | copy-start | bytes 9437188
  (17 other events, 57.3 us)
Sparse Core Ops, SparseCore 0:
  90.6 111.9 all-gather.8
  249.4 94.1 all-gather.10
  392.2 94.2 all-gather.12
  530.4 94.1 all-gather.14
